TPU v7x, 32 devices: a whole 2x2x4 slice. The times are simulated.
32 devices in a mesh: dp: 8 (over y, x, core), seq: 4 (over z).
Axes of the slice: x: 2, y: 2, z: 4, core: 2. Of those that a mesh axis runs over, the one named last changes fastest.
Arguments:
- tokens: bfloat16 [32, 1024, 576], P('dp', 'seq'), may hold values from -6 to 6
- lengths: int32 [32], P('dp'), may hold values from 256 to 1024, as said below
- w_query: bfloat16 [576, 576], replicated, may hold values from -0.25 to 0.25
- w_key: bfloat16 [576, 192], replicated, may hold values from -0.25 to 0.25
- w_value: bfloat16 [576, 192], replicated, may hold values from -0.25 to 0.25
- w_out: bfloat16 [576, 576], replicated, may hold values from -1 to 1
- w_gate: bfloat16 [576, 1536], replicated, may hold values from -0.25 to 0.25
- w_up: bfloat16 [576, 1536], replicated, may hold values from -0.25 to 0.25
- w_down: bfloat16 [1536, 576], replicated, may hold values from -0.15625 to 0.15625
- gain_attn: float32 [576], replicated, may hold values from 0.1 to 1.9
- gain_ffn: float32 [576], replicated, may hold values from 0.1 to 1.9
- cotangent: bfloat16 [32, 1024, 576], P('dp', 'seq'), may hold values from -6 to 6
Outputs:
- mixed: bfloat16 [32, 1024, 576], P('dp', 'seq')
- tokens_grad: bfloat16 [32, 1024, 576], P('dp', 'seq')
- w_query_grad: float32 [576, 576], replicated
- w_key_grad: float32 [576, 192], replicated
- w_value_grad: float32 [576, 192], replicated
- w_out_grad: float32 [576, 576], replicated
- w_gate_grad: float32 [576, 1536], replicated
- w_up_grad: float32 [576, 1536], replicated
- w_down_grad: float32 [1536, 576], replicated
- gain_attn_grad: float32 [576], replicated
- gain_ffn_grad: float32 [576], replicated
Inputs may be any that keep to these rules, and one draw needn't show every extreme that they name: A row's real tokens are its first lengths entries; among the 4 rows of each index of dp one row has exactly 1024.
All inputs are finite; a program needn't handle non-finite values.
Results may differ from a plain program's by a relative error of at most 0.03.
Values may be sent and summed in bfloat16 or wider, within the bound.
No kernel may reach another device: no remote copies, remote signals or barrier semaphores. Data moves between devices by JAX's collectives and lax.ppermute only.
A program may use at most 128 MiB of HBM per device.

v0:
```python
from functools import partial
import math

import jax
import jax.numpy as jnp
from jax import lax
from jax.sharding import PartitionSpec as P

HQ = 9
HK = 3
DH = 64


eps_norm = 1e-05
rope_base = 100000.0
neg_large = -1e30


def norm_rows(values, gain_vec):
    return (
        values * lax.rsqrt(jnp.mean(values * values, axis=-1, keepdims=True) + eps_norm) * gain_vec
    )


def rotate(values, positions, turn_sign):
    half_dim = values.shape[-1] // 2
    frequency = rope_base ** (-jnp.arange(half_dim, dtype=jnp.float32) / half_dim)
    angles = turn_sign * positions.astype(jnp.float32)[:, None] * frequency[None, :]
    cosine = jnp.cos(angles)[:, None, :]
    sine_part = jnp.sin(angles)[:, None, :]
    first_half = values[..., :half_dim]
    second_half = values[..., half_dim:]
    return jnp.concatenate(
        [
            first_half * cosine - second_half * sine_part,
            second_half * cosine + first_half * sine_part,
        ],
        axis=-1,
    )


def inner_rows(left, right):
    return lax.dot_general(
        left, right, (((0,), (0,)), ((), ())), preferred_element_type=jnp.float32
    )


def times_t(left, right):
    return lax.dot_general(
        left, right, (((1,), (1,)), ((), ())), preferred_element_type=jnp.float32
    )


def fold_piece(block_len, step_fn, carry, pieces):
    piece_count = pieces.shape[1] // block_len

    def inner_step(index_step, state):
        part_piece = lax.dynamic_slice_in_dim(pieces, index_step * block_len, block_len, 1)
        return step_fn(state, part_piece, index_step * block_len)

    return lax.fori_loop(0, piece_count, inner_step, carry)


def local(
    tokens,
    lengths,
    w_query,
    w_key,
    w_value,
    w_out,
    w_gate,
    w_up,
    w_down,
    gain_attn,
    gain_ffn,
    cotangent,
):
    row_count, block_len, model_width = tokens.shape
    group_size = HQ // HK
    kv_width = HK * DH
    score_scale = 1.0 / math.sqrt(DH)
    seq_devices = lax.axis_size("seq")
    my_start = lax.axis_index("seq") * block_len
    positions = my_start + jnp.arange(block_len, dtype=jnp.int32)
    longest = jnp.max(lengths)
    live_rows = positions[None, :] < lengths[:, None]
    query_active = my_start < longest
    inputs = tokens.reshape(-1, model_width).astype(jnp.float32)
    attn_norm, attn_pull = jax.vjp(norm_rows, inputs, gain_attn)
    attn_in = attn_norm.astype(jnp.bfloat16)
    query_pre = jnp.dot(attn_in, w_query, preferred_element_type=jnp.float32)
    query_heads = rotate(query_pre.reshape(row_count, block_len, HQ, DH), positions, 1.0).astype(
        jnp.bfloat16
    )
    query_heads = query_heads.reshape(row_count, block_len, HK, group_size, DH)
    key_pre = jnp.dot(attn_in, w_key, preferred_element_type=jnp.float32)
    key_heads = rotate(key_pre.reshape(row_count, block_len, HK, DH), positions, 1.0).astype(
        jnp.bfloat16
    )
    value_heads = jnp.dot(attn_in, w_value, preferred_element_type=jnp.float32).astype(jnp.bfloat16)
    key_value = jnp.concatenate(
        [
            key_heads.reshape(row_count, block_len, kv_width),
            value_heads.reshape(row_count, block_len, kv_width),
        ],
        axis=-1,
    )

    def allowed_for(piece_start):
        key_pos = piece_start + jnp.arange(block_len, dtype=jnp.int32)
        causal = key_pos[None, None, :] <= positions[None, :, None]
        inside = key_pos[None, None, :] < lengths[:, None, None]
        return causal & inside

    def needed_for(piece_start):
        return (piece_start <= my_start) & (piece_start < longest) & query_active

    def split_piece(pieces):
        key_part = pieces[..., :kv_width].reshape(row_count, block_len, HK, DH)
        value_part = pieces[..., kv_width:].reshape(row_count, block_len, HK, DH)
        return (key_part, value_part)

    def forward_block(carry, pieces, piece_start):

        def forward_compute_block(state):
            row_max, row_total, weighted = state
            key_part, value_part = split_piece(pieces)
            scores = (
                jnp.einsum(
                    "rqhgd,rkhd->rhgqk", query_heads, key_part, preferred_element_type=jnp.float32
                )
                * score_scale
            )
            allowed = allowed_for(piece_start)[:, None, None]
            scores = jnp.where(allowed, scores, neg_large)
            new_max = jnp.maximum(row_max, jnp.max(scores, axis=-1))
            shrink = jnp.exp(row_max - new_max)
            exp_scores = jnp.where(allowed, jnp.exp(scores - new_max[..., None]), 0.0)
            row_total = row_total * shrink + jnp.sum(exp_scores, axis=-1)
            update = jnp.einsum(
                "rhgqk,rkhd->rqhgd",
                exp_scores.astype(jnp.bfloat16),
                value_part,
                preferred_element_type=jnp.float32,
            )
            weighted = weighted * jnp.moveaxis(shrink, 3, 1)[..., None] + update
            return (new_max, row_total, weighted)

        return lax.cond(needed_for(piece_start), forward_compute_block, lambda state: state, carry)

    stat_shape = (row_count, HK, group_size, block_len)
    forward_init = (
        jnp.full(stat_shape, neg_large, jnp.float32),
        jnp.zeros(stat_shape, jnp.float32),
        jnp.zeros((row_count, block_len, HK, group_size, DH), jnp.float32),
    )
    forward_state = fold_piece(
        block_len, forward_block, forward_init, lax.all_gather(key_value, "seq", axis=1, tiled=True)
    )
    row_max, row_total, weighted = forward_state
    safe_total = jnp.where(row_total > 0, row_total, 1.0)
    attn_heads = weighted / jnp.moveaxis(safe_total, 3, 1)[..., None]
    attn_heads = jnp.where(live_rows[:, :, None, None, None], attn_heads, 0.0)
    log_sum = jnp.where(live_rows[:, None, None, :], row_max + jnp.log(safe_total), 0.0)
    attn_low = attn_heads.reshape(-1, HQ * DH).astype(jnp.bfloat16)
    residual = inputs + jnp.dot(attn_low, w_out, preferred_element_type=jnp.float32)
    ffn_norm, ffn_pull = jax.vjp(norm_rows, residual, gain_ffn)
    ffn_in = ffn_norm.astype(jnp.bfloat16)
    gate_proj = jnp.dot(ffn_in, w_gate, preferred_element_type=jnp.float32)
    up_proj = jnp.dot(ffn_in, w_up, preferred_element_type=jnp.float32)
    product, swiglu_pull = jax.vjp(
        lambda gate_in, up_in: jax.nn.silu(gate_in) * up_in, gate_proj, up_proj
    )
    hidden = product.astype(jnp.bfloat16)
    branch = jnp.dot(hidden, w_down, preferred_element_type=jnp.float32)
    mixed = (residual + branch).astype(jnp.bfloat16).reshape(row_count, block_len, model_width)
    out_low = cotangent.reshape(-1, model_width)
    out_grad = out_low.astype(jnp.float32)
    w_down_grad = inner_rows(hidden, out_low)
    hidden_grad = times_t(out_low, w_down)
    gate_grad, up_grad = swiglu_pull(hidden_grad)
    gate_low = gate_grad.astype(jnp.bfloat16)
    up_low = up_grad.astype(jnp.bfloat16)
    w_gate_grad = inner_rows(ffn_in, gate_low)
    w_up_grad = inner_rows(ffn_in, up_low)
    ffn_in_grad = times_t(gate_low, w_gate) + times_t(up_low, w_up)
    residual_part, gain_ffn_grad = ffn_pull(ffn_in_grad)
    residual_grad = out_grad + residual_part
    residual_low = residual_grad.astype(jnp.bfloat16)
    w_out_grad = inner_rows(attn_low, residual_low)
    attended_grad = times_t(residual_low, w_out).reshape(row_count, block_len, HK, group_size, DH)
    attended_grad = jnp.where(live_rows[:, :, None, None, None], attended_grad, 0.0).astype(
        jnp.bfloat16
    )
    grad_dot = jnp.moveaxis(jnp.sum(attended_grad.astype(jnp.float32) * attn_heads, axis=-1), 1, 3)

    def backward_block(with_kv, carry, pieces, piece_start):

        def backward_compute_block(state):
            key_part, value_part = split_piece(pieces)
            scores = (
                jnp.einsum(
                    "rqhgd,rkhd->rhgqk", query_heads, key_part, preferred_element_type=jnp.float32
                )
                * score_scale
            )
            allowed = allowed_for(piece_start)[:, None, None]
            weights_now = jnp.where(allowed, jnp.exp(scores - log_sum[..., None]), 0.0)
            weights_grad = jnp.einsum(
                "rqhgd,rkhd->rhgqk", attended_grad, value_part, preferred_element_type=jnp.float32
            )
            score_grad = (weights_now * (weights_grad - grad_dot[..., None])).astype(jnp.bfloat16)
            query_grad = (
                state[0]
                + jnp.einsum(
                    "rhgqk,rkhd->rqhgd", score_grad, key_part, preferred_element_type=jnp.float32
                )
                * score_scale
            )
            kv_grad = state[1]
            values_grad = jnp.einsum(
                "rhgqk,rqhgd->rkhd",
                weights_now.astype(jnp.bfloat16),
                attended_grad,
                preferred_element_type=jnp.float32,
            )
            keys_grad = (
                jnp.einsum(
                    "rhgqk,rqhgd->rkhd", score_grad, query_heads, preferred_element_type=jnp.float32
                )
                * score_scale
            )
            local_kv = jnp.concatenate(
                [
                    keys_grad.reshape(row_count, block_len, kv_width),
                    values_grad.reshape(row_count, block_len, kv_width),
                ],
                axis=-1,
            )
            current = lax.dynamic_slice_in_dim(kv_grad, piece_start, block_len, 1)
            kv_grad = lax.dynamic_update_slice_in_dim(kv_grad, current + local_kv, piece_start, 1)
            return (query_grad, kv_grad)

        return lax.cond(needed_for(piece_start), backward_compute_block, lambda state: state, carry)

    query_zero = jnp.zeros((row_count, block_len, HK, group_size, DH), jnp.float32)
    backward_init = (
        query_zero,
        jnp.zeros((row_count, block_len * seq_devices, 2 * kv_width), jnp.float32),
    )
    step_back = partial(backward_block, True)
    backward_state = fold_piece(
        block_len, step_back, backward_init, lax.all_gather(key_value, "seq", axis=1, tiled=True)
    )
    query_grad = backward_state[0]
    own_kv_grad = lax.psum_scatter(
        backward_state[1].astype(jnp.bfloat16), "seq", scatter_dimension=1, tiled=True
    ).astype(jnp.float32)
    query_low = (
        rotate(query_grad.reshape(row_count, block_len, HQ, DH), positions, -1.0)
        .astype(jnp.bfloat16)
        .reshape(-1, HQ * DH)
    )
    key_low = (
        rotate(own_kv_grad[..., :kv_width].reshape(row_count, block_len, HK, DH), positions, -1.0)
        .astype(jnp.bfloat16)
        .reshape(-1, kv_width)
    )
    value_low = own_kv_grad[..., kv_width:].astype(jnp.bfloat16).reshape(-1, kv_width)
    w_query_grad = inner_rows(attn_in, query_low)
    w_key_grad = inner_rows(attn_in, key_low)
    w_value_grad = inner_rows(attn_in, value_low)
    attn_in_grad = (
        times_t(query_low, w_query) + times_t(key_low, w_key) + times_t(value_low, w_value)
    )
    inputs_part, gain_attn_grad = attn_pull(attn_in_grad)
    tokens_grad = (
        (residual_grad + inputs_part)
        .astype(jnp.bfloat16)
        .reshape(row_count, block_len, model_width)
    )
    (
        w_query_grad,
        w_key_grad,
        w_value_grad,
        w_out_grad,
        w_gate_grad,
        w_up_grad,
        w_down_grad,
        gain_attn_grad,
        gain_ffn_grad,
    ) = lax.psum(
        (
            w_query_grad,
            w_key_grad,
            w_value_grad,
            w_out_grad,
            w_gate_grad,
            w_up_grad,
            w_down_grad,
            gain_attn_grad,
            gain_ffn_grad,
        ),
        ("dp", "seq"),
    )
    return (
        mixed,
        tokens_grad,
        w_query_grad,
        w_key_grad,
        w_value_grad,
        w_out_grad,
        w_gate_grad,
        w_up_grad,
        w_down_grad,
        gain_attn_grad,
        gain_ffn_grad,
    )


def solution(mesh):
    return jax.shard_map(
        local,
        mesh=mesh,
        in_specs=(
            P("dp", "seq", None),
            P("dp"),
            P(),
            P(),
            P(),
            P(),
            P(),
            P(),
            P(),
            P(),
            P(),
            P("dp", "seq", None),
        ),
        out_specs=(
            P("dp", "seq", None),
            P("dp", "seq", None),
            P(),
            P(),
            P(),
            P(),
            P(),
            P(),
            P(),
            P(),
            P(),
        ),
        check_vma=False,
    )
```

profile of v0, /device:TPU:0, one launch (start us, length us, event | category | flops | bytes accessed | tf_op | source)
XLA Modules:
  0.0 584.7 jit_solution(18100267050135279804)
XLA Ops:
  17.6 2.3 copy.40
  19.9 2.5 copy.71
  24.1 58.3 %all-gather.2.cloned.1.call-done = bf16[4,1024,384]{1,2,0:T(8,128)(2,1)} async-done(((bf16[4,256,384]{1,2,0:T(8,128)(2,1)}), bf16[4,1024,384]{1,2,0:T(8,128)(2,1)}) %all-gather.2.cloned.1.call-update) | async-done | bytes 3145744 | tf_op jit(solution)/shard_map/all_gather | solution.py:158
  84.2 13.1 %while.36 = (s32[]{:T(128)}, f32[4,3,3,256]{3,2,1,0:T(4,128)S(1)}, f32[4,3,3,256]{3,2,1,0:T(4,128)S(1)}, f32[4,256,3,3,64]{1,4,3,2,0:T(8,128)}, s32[]{:T(128)}, ...) while((s32[]{:T(128)}, f32[4,3,3,256]{3,2,1,0:T(4,128)S(1)}, ...), condition=%wide.region_7.8_spmd.clone.clone, body=%wide.region_2.7_spmd.clone.clone.sunk | while | flops 636187136 | bytes 57222560 | solution.py:61
  84.8 10.0 %conditional.8 = ((f32[4,3,3,256]{3,2,1,0:T(4,128)S(1)}, f32[4,3,3,256]{3,2,1,0:T(4,128)S(1)}, f32[4,256,3,3,64]{1,4,3,2,0:T(8,128)})) conditional(s32[]{:T(128)} %convert_element_type.237, (f32[4,3,3,256]{3,2,1,0:T(4,128)S(1)}, f32[4,3,3,256]{3,2,1,0:T(4,128)S(1)}, f32[4,256,3,3,64]{1,4,3,2,0:T(8,128)}) %tuple.135, (s32[]{:T(128)}, s32[]{:T(128)}, ...), branch_computations={%region_3.0_spmd, %region_4.6_spmd} | conditional | flops 636187136 | bytes 57221284 | solution.py:149
  88.1 2.5 fusion.6
  90.6 2.7 bitcast_add_fusion
  102.7 2.0 copy-done.54
  104.7 2.7 fusion.66
  107.4 2.7 fusion.65
  110.1 7.2 %multiply_convert_fusion = (bf16[1024,1536]{1,0:T(8,128)(2,1)S(1)}, bf16[1024,1536]{1,0:T(8,128)(2,1)}, bf16[1024,1536]{1,0:T(8,128)(2,1)}) fusion(f32[1024,1536]{1,0:T(8,128)S(1)} %fusion.65, f32[1024,1536]{1,0:T(8,128)S(1)} %fusion.66, bf16[1024,576]{0,1:T(8,128)(2,1)S(1)} %bitcast.202, bf16[1536,576]{0,1:T(8,128)(2,1)S(1)} %copy-done), kind=kOutput, calls=%fused_computation.50 | convolution fusion | flops 1837105152 | bytes 24969216 | tf_op jit(solution)/shard_map/dot_general | solution.py:49
  117.3 5.0 fusion.67
  122.4 2.4 multiply_reduce_fusion
  126.9 2.1 fusion.48
  129.0 3.5 reshape.529
  132.4 3.6 multiply_reduce_fusion.3
  137.7 3.5 broadcast_in_dim.114
  141.2 17.4 %while.37 = (s32[]{:T(128)}, f32[4,256,3,3,64]{1,4,3,2,0:T(8,128)}, f32[4,1024,384]{1,2,0:T(8,128)}, s32[]{:T(128)}, s32[]{:T(128)}, /*index=5*/pred[]{:T(512)},...) while((s32[]{:T(128)}, f32[4,256,3,3,64]{1,4,3,2,0:T(8,128)}, ...), condition=%wide.region_14.15_spmd.clone.clone, body=%wide.region_11.14_spmd.clone.clone.sunk | while | flops 1536034304 | bytes 85579216 | solution.py:61
  141.9 14.7 %conditional.9 = ((f32[4,256,3,3,64]{1,4,3,2,0:T(8,128)}, f32[4,1024,384]{1,2,0:T(8,128)})) conditional(s32[]{:T(128)} %convert_element_type.238, (f32[4,256,3,3,64]{1,4,3,2,0:T(8,128)}, f32[4,1024,384]{1,2,0:T(8,128)}) %tuple.138, (s32[]{:T(128)}, s32[]{:T(128)}, s32[4]{0:T(128)S(1)}, bf16[4,1024,384]{1,2,0:T(8,128)(2,1)}, ...), branch_computations={%region_12.12_spmd, %region_13.13_spmd} | conditional | flops 1536034304 | bytes 85577912 | solution.py:244
  147.0 3.1 fusion.17
  152.8 3.7 fusion.24
  158.6 5.0 convert_element_type.168
  170.8 2.2 fusion.70
  173.7 2.2 fusion.46
  176.4 3.8 fusion.73
  180.1 3.8 fusion.72
  183.9 3.8 fusion.74
  187.7 107.9 %reduce-scatter.2.cloned.1.call-done = bf16[4,256,384]{1,2,0:T(8,128)(2,1)} async-done(((bf16[4,1024,384]{1,2,0:T(8,128)(2,1)}), bf16[4,256,384]{1,2,0:T(8,128)(2,1)}) %reduce-scatter.2.cloned.1.call-update) | async-done | bytes 786448 | tf_op jit(solution)/shard_map/reduce_scatter | solution.py:256
  301.7 4.9 add_convert_fusion
  314.6 42.0 %all-reduce = (f32[576]{0:T(1024)}, f32[576]{0:T(1024)}) all-reduce(f32[576]{0:T(1024)S(1)} %get-tuple-element.758, f32[576]{0:T(1024)S(1)} %get-tuple-element.756), channel_id=1, replica_groups=mesh['dp'=8,'seq'=4] {'dp','seq'}, use_global_device_ids=true, to_apply=%region_25.26 | all-reduce | flops 1152 | bytes 9216 | tf_op jit(solution)/shard_map/psum | solution.py:292
  356.6 207.3 %all-reduce.4.cloned.1.call-done = (f32[576,576]{1,0:T(8,128)}, f32[576,192]{0,1:T(8,128)}, f32[576,192]{0,1:T(8,128)}, f32[576,576]{1,0:T(8,128)}, f32[576,1536...) async-done(((f32[576,576]{1,0:T(8,128)}, f32[576,192]{0,1:T(8,128)}, f32[576,192]{0,1:T(8,128)}, f32[576,576]{1,0:T(8,128)}, f32[576,1536]{1,0:T(8,128)}, ...) | async-done | bytes 14155792 | tf_op jit(solution)/shard_map/psum | solution.py:292
  563.9 2.7 copy.137
  (217 shorter events, 67.6 us)
Async XLA Ops:
  7.2 102.9 %copy-start = (bf16[1536,576]{0,1:T(8,128)(2,1)S(1)}, bf16[1536,576]{0,1:T(8,128)(2,1)}, u32[]{:S(2)}) copy-start(bf16[1536,576]{0,1:T(8,128)(2,1)} %param.28) | copy-start | bytes 5308420
  7.2 75.3 %all-gather.2.cloned.1.call-start = ((), (), s32[]{:S(2)}) async-start(), calls=%async_computation.1 | async-start | bytes 3932160 | tf_op jit(solution)/shard_map/all_gather | solution.py:158
  10.4 12.0 %copy-start.51 = (f32[4,256]{1,0:T(4,128)}, f32[4,256]{1,0:T(4,128)S(1)}, u32[]{:S(2)}) copy-start(f32[4,256]{1,0:T(4,128)S(1)} %get-tuple-element.846) | copy-start | bytes 12292
  11.4 2.8 copy-start.4
  16.2 279.5 %reduce-scatter.2.cloned.1.call-start = ((), (), s32[]{:S(2)}) async-start(), calls=%async_computation.2 | async-start | bytes 3932160 | tf_op jit(solution)/shard_map/reduce_scatter | solution.py:256
  19.9 2.5 copy-start.36
  88.1 2.5 copy-start.7
  102.4 22.4 %copy-start.12 = (f32[1024,576]{0,1:T(8,128)}, f32[1024,576]{0,1:T(8,128)S(1)}, u32[]{:S(2)}) copy-start(f32[1024,576]{0,1:T(8,128)S(1)} %get-tuple-element.855) | copy-start | bytes 7077892
  102.4 2.3 copy-start.54
  104.7 2.7 copy-start.29
  104.7 2.7 copy-start.53
  107.4 2.7 copy-start.17
  117.3 5.1 copy-start.55
  152.8 3.8 copy-start.2
  163.6 400.3 %all-reduce.4.cloned.1.call-start = ((), (), s32[]{:S(2)}) async-start(), calls=%async_computation.3 | async-start | bytes 29097984 | tf_op jit(solution)/shard_map/psum | solution.py:292
  165.3 5.4 copy-start.19
  170.8 2.9 copy-start.16
  173.7 2.6 copy-start.56
  176.3 3.8 copy-start.58
  180.1 3.8 copy-start.18
  180.1 3.8 copy-start.57
  297.7 2.6 copy-start.34
  308.0 2.3 copy-start.6
  308.0 3.0 copy-start.22
  308.0 3.2 copy-start.26
  308.0 3.2 copy-start.46
  563.9 2.7 copy-start.38
  563.9 3.5 copy-start.37
  563.9 4.3 copy-start.28
  566.7 2.7 copy-start.25
  569.3 3.3 copy-start.24
  572.6 3.3 copy-start.23
  (30 other events, 44.4 us)
Sparse Core Ops, SparseCore 0:
  16.3 66.1 all-gather.1
  163.7 131.8 reduce-scatter.1
  303.3 260.6 all-reduce.3
where the time goes:
time: 593 us; the launch traced here: 585 us
  waiting for transfers between devices  374 us (63%)
  matrix products  65.3 us (11%)
  local copies, waits for them, and re-layouts  52.4 us (9%)
  blocking collectives  42 us (7%)
  other arithmetic  29.4 us (5%)
  between operations  15.5 us (3%)
  loops' own time  6.07 us (1%)
    psum x1, waiting for transfers between devices, local(): lax.psum((w_query_grad, w_key_grad, w_value_grad, w_out_grad, w_gate_grad...  207 us
    reduce_scatter x1, waiting for transfers between devices, local(): lax.psum_scatter(backward_state[1].astype(jnp.bfloat16), 'seq', scatter_d...  108 us
    all_gather x1, waiting for transfers between devices, local(): lax.all_gather(key_value, 'seq', axis=1, tiled=True)  58.3 us
    psum x1, blocking collectives, local(): lax.psum((w_query_grad, w_key_grad, w_value_grad, w_out_grad, w_gate_grad...  42 us
    unnamed x120, local copies, waits for them, and re-layouts  29.7 us
    dot_general x7, matrix products, times_t(): lax.dot_general(left, right, (((1,), (1,)), ((), ())), preferred_element_...  19.5 us
    dot_general x7, matrix products, inner_rows(): lax.dot_general(left, right, (((0,), (0,)), ((), ())), preferred_element_...  18.7 us
  transfers between devices with their start and end apart: 3, of which 3 were waited for; matrix products, arithmetic and copies ran while one was open for 6% of the time, Pallas kernels for 0%

commit v1 on v0

--- a/solution.py
+++ b/solution.py
@@ -4,6 +4,8 @@
 import jax
 import jax.numpy as jnp
 from jax import lax
+from jax.experimental import pallas as pl
+from jax.experimental.pallas import tpu as pltpu
 from jax.sharding import PartitionSpec as P
 
 HQ = 9
@@ -61,7 +63,7 @@
     return lax.fori_loop(0, piece_count, inner_step, carry)
 
 
-def local(
+def local_general(
     tokens,
     lengths,
     w_query,
@@ -318,9 +320,401 @@
     )
 
 
+GROUP = HQ // HK
+QBLK = 256
+
+
+def mul_nt(left, right):
+    return lax.dot_general(
+        left, right, (((1,), (1,)), ((), ())), preferred_element_type=jnp.float32
+    )
+
+
+def mul_nn(left, right):
+    return lax.dot_general(
+        left, right, (((1,), (0,)), ((), ())), preferred_element_type=jnp.float32
+    )
+
+
+def turn(values, cosine, sine_part):
+    first_half, second_half = values[: DH // 2], values[DH // 2 :]
+    return jnp.concatenate(
+        [
+            first_half * cosine - second_half * sine_part,
+            second_half * cosine + first_half * sine_part,
+        ],
+        axis=0,
+    )
+
+
+def causal_mask():
+    key_at = lax.broadcasted_iota(jnp.int32, (QBLK, QBLK), 0)
+    query_at = lax.broadcasted_iota(jnp.int32, (QBLK, QBLK), 1)
+    return jnp.concatenate([key_at <= query_at] * GROUP, axis=1)
+
+
+def heads_of(ref, cols):
+    return jnp.concatenate([ref[j * DH : (j + 1) * DH, cols] for j in range(GROUP)], axis=1)
+
+
+def attend_kernel(
+    length_ref,
+    attn_in_ref,
+    weights_ref,
+    cos_ref,
+    sin_ref,
+    query_ref,
+    key_ref,
+    value_ref,
+    out_ref,
+    lse_ref,
+    key_rows,
+):
+    seq_len = attn_in_ref.shape[0]
+    attn_in = attn_in_ref[...]
+    cosine, sine_part = cos_ref[...], sin_ref[...]
+    for j in range(GROUP):
+        pre = mul_nt(weights_ref[0, j * DH : (j + 1) * DH], attn_in)
+        query_ref[j * DH : (j + 1) * DH] = (turn(pre, cosine, sine_part) * DH**-0.5).astype(
+            jnp.bfloat16
+        )
+    pre = mul_nt(weights_ref[0, GROUP * DH : (GROUP + 1) * DH], attn_in)
+    keys = turn(pre, cosine, sine_part).astype(jnp.bfloat16)
+    key_ref[...] = keys
+    key_rows[...] = keys.T
+    value_ref[...] = mul_nt(weights_ref[0, (GROUP + 1) * DH :], attn_in).astype(jnp.bfloat16)
+    mask = causal_mask()
+    for at in range(seq_len // QBLK):
+        cols = slice(at * QBLK, (at + 1) * QBLK)
+        queries = heads_of(query_ref, cols)
+        scores, top = [], None
+        for k in range(at + 1):
+            part = mul_nn(key_rows[k * QBLK : (k + 1) * QBLK], queries)
+            if k == at:
+                part = jnp.where(mask, part, neg_large)
+            scores.append(part)
+            part_top = jnp.max(part, axis=0, keepdims=True)
+            top = part_top if top is None else jnp.maximum(top, part_top)
+        total, weighted = 0.0, 0.0
+        for k in range(at + 1):
+            weights_now = jnp.exp(scores[k] - top)
+            total = total + jnp.sum(weights_now, axis=0, keepdims=True)
+            weighted = weighted + mul_nn(
+                value_ref[:, k * QBLK : (k + 1) * QBLK], weights_now.astype(jnp.bfloat16)
+            )
+        weighted = weighted * (1.0 / total)
+        log_sum = top + jnp.log(total)
+        place = at * QBLK + lax.broadcasted_iota(jnp.int32, (1, QBLK), 1)
+        for j in range(GROUP):
+            mine = slice(j * QBLK, (j + 1) * QBLK)
+            out_ref[j * DH : (j + 1) * DH, cols] = jnp.where(
+                place < length_ref[0], weighted[:, mine], 0.0
+            ).astype(jnp.bfloat16)
+            lse_ref[0, j : j + 1, cols] = log_sum[:, mine]
+
+
+def attend_back_kernel(
+    query_ref,
+    key_ref,
+    value_ref,
+    out_ref,
+    out_grad_ref,
+    lse_ref,
+    cos_ref,
+    sin_ref,
+    query_grad_ref,
+    key_grad_ref,
+    value_grad_ref,
+    key_rows,
+    value_rows,
+    key_sum,
+    value_sum,
+):
+    key_rows[...] = key_ref[...].T
+    value_rows[...] = value_ref[...].T
+    blocks = query_ref.shape[1] // QBLK
+    mask = causal_mask()
+    for at in reversed(range(blocks)):
+        cols = slice(at * QBLK, (at + 1) * QBLK)
+        queries, out_grad = heads_of(query_ref, cols), heads_of(out_grad_ref, cols)
+        grad_dot = jnp.sum(
+            out_grad.astype(jnp.float32) * heads_of(out_ref, cols).astype(jnp.float32),
+            axis=0,
+            keepdims=True,
+        )
+        log_sum = jnp.concatenate([lse_ref[0, j : j + 1, cols] for j in range(GROUP)], axis=1)
+        query_grad = 0.0
+        for k in range(at + 1):
+            own = slice(k * QBLK, (k + 1) * QBLK)
+            weights_now = jnp.exp(mul_nn(key_rows[own], queries) - log_sum)
+            if k == at:
+                weights_now = jnp.where(mask, weights_now, 0.0)
+            weights_grad = mul_nn(value_rows[own], out_grad)
+            score_grad = (weights_now * (weights_grad - grad_dot)).astype(jnp.bfloat16)
+            value_part = mul_nt(out_grad, weights_now.astype(jnp.bfloat16))
+            key_part = mul_nt(queries, score_grad)
+            if at == blocks - 1:
+                value_sum[:, own] = value_part
+                key_sum[:, own] = key_part
+            else:
+                value_sum[:, own] += value_part
+                key_sum[:, own] += key_part
+            query_grad = query_grad + mul_nn(key_ref[:, own], score_grad)
+        cosine, sine_part = cos_ref[:, cols] * DH**-0.5, sin_ref[:, cols] * -(DH**-0.5)
+        for j in range(GROUP):
+            query_grad_ref[j * DH : (j + 1) * DH, cols] = turn(
+                query_grad[:, j * QBLK : (j + 1) * QBLK], cosine, sine_part
+            ).astype(jnp.bfloat16)
+    key_grad_ref[...] = turn(key_sum[...], cos_ref[...], -sin_ref[...]).astype(jnp.bfloat16)
+    value_grad_ref[...] = value_sum[...].astype(jnp.bfloat16)
+
+
+def attend_specs(seq_len):
+    query_spec = pl.BlockSpec((GROUP * DH, seq_len), lambda h: (h, 0))
+    key_spec = pl.BlockSpec((DH, seq_len), lambda h: (h, 0))
+    lse_spec = pl.BlockSpec((1, 8, seq_len), lambda h: (h, 0, 0))
+    angle_spec = pl.BlockSpec((DH // 2, seq_len), lambda h: (0, 0))
+    return query_spec, key_spec, lse_spec, angle_spec
+
+
+def attend(length, attn_in, weights, cosine, sine_part):
+    seq_len, width = attn_in.shape
+    query_spec, key_spec, lse_spec, angle_spec = attend_specs(seq_len)
+    head_rows = (GROUP + 2) * DH
+    return pl.pallas_call(
+        attend_kernel,
+        grid=(HK,),
+        in_specs=[
+            pl.BlockSpec(memory_space=pltpu.SMEM),
+            pl.BlockSpec((seq_len, width), lambda h: (0, 0)),
+            pl.BlockSpec((1, head_rows, width), lambda h: (h, 0, 0)),
+            angle_spec,
+            angle_spec,
+        ],
+        out_specs=[query_spec, key_spec, key_spec, query_spec, lse_spec],
+        out_shape=[
+            jax.ShapeDtypeStruct((HQ * DH, seq_len), jnp.bfloat16),
+            jax.ShapeDtypeStruct((HK * DH, seq_len), jnp.bfloat16),
+            jax.ShapeDtypeStruct((HK * DH, seq_len), jnp.bfloat16),
+            jax.ShapeDtypeStruct((HQ * DH, seq_len), jnp.bfloat16),
+            jax.ShapeDtypeStruct((HK, 8, seq_len), jnp.float32),
+        ],
+        scratch_shapes=[pltpu.VMEM((seq_len, DH), jnp.bfloat16)],
+        compiler_params=pltpu.CompilerParams(vmem_limit_bytes=40 * 2**20),
+        cost_estimate=pl.CostEstimate(
+            flops=20 * 10**9, bytes_accessed=8 * 2**20, transcendentals=6 * 10**6
+        ),
+        name="attend",
+    )(length, attn_in, weights, cosine, sine_part)
+
+
+def attend_back(queries, keys, values, attended, attended_grad, log_sum, cosine, sine_part):
+    seq_len = queries.shape[1]
+    query_spec, key_spec, lse_spec, angle_spec = attend_specs(seq_len)
+    return pl.pallas_call(
+        attend_back_kernel,
+        grid=(HK,),
+        in_specs=[
+            query_spec,
+            key_spec,
+            key_spec,
+            query_spec,
+            query_spec,
+            lse_spec,
+            angle_spec,
+            angle_spec,
+        ],
+        out_specs=[query_spec, key_spec, key_spec],
+        out_shape=[
+            jax.ShapeDtypeStruct((HQ * DH, seq_len), jnp.bfloat16),
+            jax.ShapeDtypeStruct((HK * DH, seq_len), jnp.bfloat16),
+            jax.ShapeDtypeStruct((HK * DH, seq_len), jnp.bfloat16),
+        ],
+        scratch_shapes=[pltpu.VMEM((seq_len, DH), jnp.bfloat16)] * 2
+        + [pltpu.VMEM((DH, seq_len), jnp.float32)] * 2,
+        compiler_params=pltpu.CompilerParams(vmem_limit_bytes=40 * 2**20),
+        cost_estimate=pl.CostEstimate(
+            flops=25 * 10**9, bytes_accessed=8 * 2**20, transcendentals=6 * 10**6
+        ),
+        name="attend_back",
+    )(queries, keys, values, attended, attended_grad, log_sum, cosine, sine_part)
+
+
+def swap(values, axis, bits, count):
+    return lax.ppermute(values, axis, [(k, k ^ bits) for k in range(count)])
+
+
+def pick(values, index, size, axis):
+    return lax.dynamic_slice_in_dim(values, index * size, size, axis)
+
+
+def two(bit, mine, other, axis):
+    return jnp.concatenate(
+        [jnp.where(bit == 0, mine, other), jnp.where(bit == 0, other, mine)], axis=axis
+    )
+
+
+def sum_over_devices(partial_sum):
+    rows, cols = partial_sum.shape
+    dp_at, seq_at = lax.axis_index("dp"), lax.axis_index("seq")
+    core, plane, near, far = dp_at % 2, dp_at // 2, seq_at % 2, seq_at // 2
+    low = lambda v: v.astype(jnp.bfloat16)
+    wide = lambda v: v.astype(jnp.float32)
+    other = swap(low(pick(partial_sum, 1 - core, rows // 2, 0)), "dp", 1, 8)
+    half = pick(partial_sum, core, rows // 2, 0) + wide(other)
+    size = rows // 8
+    total = pick(half, plane, size, 0)
+    for step in (1, 2, 3):
+        total = total + wide(swap(low(pick(half, plane ^ step, size, 0)), "dp", 2 * step, 8))
+    size = cols // 2
+    other = swap(low(pick(total, 1 - near, size, 1)), "seq", 1, 4)
+    total = pick(total, near, size, 1) + wide(other)
+    size = cols // 4
+    other = swap(low(pick(total, 1 - far, size, 1)), "seq", 2, 4)
+    total = low(pick(total, far, size, 1) + wide(other))
+    total = two(far, total, swap(total, "seq", 2, 4), 1)
+    total = two(near, total, swap(total, "seq", 1, 4), 1)
+    parts = [total] + [swap(total, "dp", 2 * step, 8) for step in (1, 2, 3)]
+    half = []
+    for at in range(4):
+        piece = parts[3]
+        for step in (2, 1, 0):
+            piece = jnp.where(plane == at ^ step, parts[step], piece)
+        half.append(piece)
+    half = jnp.concatenate(half, axis=0)
+    return two(core, half, swap(half, "dp", 1, 8), 0).astype(jnp.float32)
+
+
+def rows_in(values):
+    count, block_len, width = values.shape
+    seq_at = lax.axis_index("seq")
+    whole = jnp.zeros((count * block_len, width), values.dtype)
+    for step in range(count):
+        chunk = lax.dynamic_index_in_dim(values, (seq_at + step) % count, 0, keepdims=False)
+        if step:
+            chunk = lax.ppermute(chunk, "seq", [(k, (k + step) % count) for k in range(count)])
+        place = (seq_at - step) % count * block_len
+        whole = lax.dynamic_update_slice_in_dim(whole, chunk, place, 0)
+    return whole
+
+
+def rows_out(whole, count):
+    block_len = whole.shape[0] // count
+    seq_at = lax.axis_index("seq")
+    values = jnp.zeros((count, block_len, whole.shape[1]), whole.dtype)
+    for step in range(count):
+        chunk = pick(whole, (seq_at + step) % count, block_len, 0)
+        if step:
+            chunk = lax.ppermute(chunk, "seq", [(k, (k + step) % count) for k in range(count)])
+        values = lax.dynamic_update_slice_in_dim(values, chunk[None], (seq_at - step) % count, 0)
+    return values
+
+
+def local_rows(
+    tokens,
+    lengths,
+    w_query,
+    w_key,
+    w_value,
+    w_out,
+    w_gate,
+    w_up,
+    w_down,
+    gain_attn,
+    gain_ffn,
+    cotangent,
+):
+    row_count, block_len, model_width = tokens.shape
+    seq_len = row_count * block_len
+    q_width, kv_width = HQ * DH, HK * DH
+    seq_at = lax.axis_index("seq")
+    length = lax.dynamic_slice_in_dim(lengths, seq_at, 1)
+    positions = jnp.arange(seq_len, dtype=jnp.int32)
+    live = positions < length
+    half_dim = DH // 2
+    frequency = rope_base ** (-jnp.arange(half_dim, dtype=jnp.float32) / half_dim)
+    angles = frequency[:, None] * positions.astype(jnp.float32)[None, :]
+    cosine, sine_part = jnp.cos(angles), jnp.sin(angles)
+    w_heads = jnp.concatenate(
+        [
+            w_query.T.reshape(HK, GROUP * DH, model_width),
+            w_key.T.reshape(HK, DH, model_width),
+            w_value.T.reshape(HK, DH, model_width),
+        ],
+        axis=1,
+    )
+    w_qkv = jnp.concatenate([w_query, w_key, w_value], axis=1)
+
+    inputs = rows_in(tokens).astype(jnp.float32)
+    out_low = rows_in(cotangent)
+    attn_norm, attn_pull = jax.vjp(norm_rows, inputs, gain_attn)
+    attn_in = attn_norm.astype(jnp.bfloat16)
+    queries, keys, values, attended, log_sum = attend(length, attn_in, w_heads, cosine, sine_part)
+    residual = inputs + inner_rows(attended, w_out)
+    ffn_norm, ffn_pull = jax.vjp(norm_rows, residual, gain_ffn)
+    ffn_in = ffn_norm.astype(jnp.bfloat16)
+    gate_proj = jnp.dot(ffn_in, w_gate, preferred_element_type=jnp.float32)
+    up_proj = jnp.dot(ffn_in, w_up, preferred_element_type=jnp.float32)
+    product, swiglu_pull = jax.vjp(
+        lambda gate_in, up_in: jax.nn.silu(gate_in) * up_in, gate_proj, up_proj
+    )
+    hidden = product.astype(jnp.bfloat16)
+    branch = jnp.dot(hidden, w_down, preferred_element_type=jnp.float32)
+    mixed = rows_out((residual + branch).astype(jnp.bfloat16), row_count)
+    out_grad = out_low.astype(jnp.float32)
+    w_down_sum = sum_over_devices(inner_rows(out_low, hidden))
+    hidden_grad = times_t(out_low, w_down)
+    gate_grad, up_grad = swiglu_pull(hidden_grad)
+    gate_low = gate_grad.astype(jnp.bfloat16)
+    up_low = up_grad.astype(jnp.bfloat16)
+    w_gate_sum = sum_over_devices(inner_rows(ffn_in, gate_low))
+    w_up_sum = sum_over_devices(inner_rows(ffn_in, up_low))
+    ffn_in_grad = times_t(gate_low, w_gate) + times_t(up_low, w_up)
+    residual_part, gain_ffn_grad = ffn_pull(ffn_in_grad)
+    residual_grad = out_grad + residual_part
+    residual_low = residual_grad.astype(jnp.bfloat16)
+    w_out_grad = jnp.dot(attended, residual_low, preferred_element_type=jnp.float32)
+    attended_grad = jnp.where(live[None, :], times_t(w_out, residual_low), 0.0).astype(
+        jnp.bfloat16
+    )
+    query_low, key_low, value_low = attend_back(
+        queries, keys, values, attended, attended_grad, log_sum, cosine, sine_part
+    )
+    qkv_low = jnp.concatenate([query_low, key_low, value_low], axis=0)
+    attn_in_grad = lax.dot_general(
+        qkv_low, w_qkv, (((0,), (1,)), ((), ())), preferred_element_type=jnp.float32
+    )
+    inputs_part, gain_attn_grad = attn_pull(attn_in_grad)
+    tokens_grad = rows_out((residual_grad + inputs_part).astype(jnp.bfloat16), row_count)
+    w_qkv_grad = lax.dot_general(
+        attn_in, qkv_low, (((0,), (1,)), ((), ())), preferred_element_type=jnp.float32
+    )
+    attn_sum = sum_over_devices(jnp.concatenate([w_qkv_grad, w_out_grad], axis=1))
+    gains = jnp.stack([gain_attn_grad, gain_ffn_grad])
+    gains_sum = gains
+    for bits in (1, 2, 4):
+        gains_sum = gains_sum + swap(gains_sum, "dp", bits, 8)
+    for bits in (1, 2):
+        gains_sum = gains_sum + swap(gains_sum, "seq", bits, 4)
+    return (
+        mixed,
+        tokens_grad,
+        attn_sum[:, :q_width],
+        attn_sum[:, q_width : q_width + kv_width],
+        attn_sum[:, q_width + kv_width : q_width + 2 * kv_width],
+        attn_sum[:, q_width + 2 * kv_width :],
+        w_gate_sum,
+        w_up_sum,
+        w_down_sum.T,
+        gains_sum[0],
+        gains_sum[1],
+    )
+
+
 def solution(mesh):
+    whole_rows = mesh.shape["dp"] == 8 and mesh.shape["seq"] == 4
     return jax.shard_map(
-        local,
+        local_rows if whole_rows else local_general,
         mesh=mesh,
         in_specs=(
             P("dp", "seq", None),

time: 593 us -> 361 us (0.61)
  waiting for transfers between devices: 374 us -> 92.5 us
  starting transfers between devices: 0.33 us -> 96.9 us
  blocking collectives: 42 us -> 0 us
  Pallas kernels: 0 us -> 31.2 us
  matrix products: 65.3 us -> 45 us
  between operations: 15.5 us -> 2.23 us
  loops' own time: 6.07 us -> 0 us
    psum x1 -> x0, waiting for transfers between devices: 207 us -> none  [local(): lax.psum((w_query_grad, w_key_grad, w_value_grad, w_out_grad, w_gate_grad...]
    reduce_scatter x1 -> x0, waiting for transfers between devices: 108 us -> none  [local(): lax.psum_scatter(backward_state[1].astype(jnp.bfloat16), 'seq', scatter_d...]
    ppermute x0 -> x65, starting transfers between devices: none -> 96.9 us  [the longest x53 61.4 us: swap(): return lax.ppermute(values, axis, [(k, k ^ bits) for k in range(count)])]
    ppermute x0 -> x65, waiting for transfers between devices: none -> 92.5 us  [the longest x53 77 us: swap(): return lax.ppermute(values, axis, [(k, k ^ bits) for k in range(count)])]
    all_gather x1 -> x0, waiting for transfers between devices: 58.3 us -> none  [local(): lax.all_gather(key_value, 'seq', axis=1, tiled=True)]
    psum x1 -> x0, blocking collectives: 42 us -> none  [local(): lax.psum((w_query_grad, w_key_grad, w_value_grad, w_out_grad, w_gate_grad...]
    pallas_call x0 -> x2, Pallas kernels: none -> 31.2 us  [the longest x1 16.2 us: attend(): pl.pallas_call(attend_kernel, grid=(HK,), in_specs=[pl.BlockSpec(memory_s...]
    unnamed x120 -> x62, local copies, waits for them, and re-layouts: 29.7 us -> 9.05 us
  transfers between devices with their start and end apart: 3 -> 65, of which waited for: 3 -> 31; matrix products, arithmetic and copies ran while one was open for 6% -> 24% of each run, Pallas kernels for 0% -> 5%
where the time goes in v1:
time: 361 us; the launch traced here: 357 us
  starting transfers between devices  96.9 us (27%)
  waiting for transfers between devices  92.5 us (26%)
  local copies, waits for them, and re-layouts  55.6 us (15%)
  matrix products  45 us (12%)
  other arithmetic  33.2 us (9%)
  Pallas kernels  31.2 us (9%)
    ppermute x53, waiting for transfers between devices, swap(): return lax.ppermute(values, axis, [(k, k ^ bits) for k in range(count)])  77 us
    ppermute x53, starting transfers between devices, swap(): return lax.ppermute(values, axis, [(k, k ^ bits) for k in range(count)])  61.4 us
    ppermute x6, starting transfers between devices, rows_out(): lax.ppermute(chunk, 'seq', [(k, (k + step) % count) for k in range(count)])  24.3 us
    dot_general x4, matrix products, times_t(): lax.dot_general(left, right, (((1,), (1,)), ((), ())), preferred_element_...  18.4 us
    pallas_call x1, Pallas kernels, attend(): pl.pallas_call(attend_kernel, grid=(HK,), in_specs=[pl.BlockSpec(memory_s...  16.2 us
    ppermute x6, waiting for transfers between devices, rows_out(): lax.ppermute(chunk, 'seq', [(k, (k + step) % count) for k in range(count)])  15.5 us
    pallas_call x1, Pallas kernels, attend_back(): pl.pallas_call(attend_back_kernel, grid=(HK,), in_specs=[query_spec, key_...  15.1 us
    dynamic_slice x9, local copies, waits for them, and re-layouts, rows_in(): lax.dynamic_index_in_dim(values, (seq_at + step) % count, 0, keepdims=False)  11.4 us
  transfers between devices with their start and end apart: 65, of which 31 were waited for; matrix products, arithmetic and copies ran while one was open for 24% of the time, Pallas kernels for 5%

profile of v1, /device:TPU:0, one launch (start us, length us, event | category | flops | bytes accessed | tf_op | source)
XLA Modules:
  0.0 356.7 jit_solution(1932995750373588749)
XLA Ops:
  5.3 3.0 collective-permute-start
  31.8 3.3 collective-permute-start.8
  42.4 16.2 %attend.1 = (bf16[576,1024]{1,0:T(8,128)(2,1)S(1)}, bf16[192,1024]{1,0:T(8,128)(2,1)S(1)}, bf16[192,1024]{1,0:T(8,128)(2,1)S(1)}, bf16[576,1024]{1,0:T(8,128)(2,1)S(1)}, f32[3,8,1024]{2,1,0:T(8,128)S(1)}) custom-call(s32[1]{0:T(128)} %dynamic_slice.176.length_ref, bf16[1024,576]{1,0:T(8,128)(2,1)S(1)} %fusion.6.attn_in_ref, ...), custom_call_target="tpu_custom_call" | custom-call | flops 20000000000 | bytes 8388608 | tf_op jit(solution)/shard_map/attend/pallas_call | solution.py:484
  61.7 4.5 %fusion.31 = f32[1024,1536]{1,0:T(8,128)} fusion(bf16[1024,576]{1,0:T(8,128)(2,1)S(1)} %multiply_convert_fusion.2, bf16[576,1536]{1,0:T(8,128)(2,1)S(1)} %copy-done.23), kind=kOutput, calls=%fused_computation.198 | convolution fusion | flops 1811939328 | bytes 9240576 | tf_op jit(solution)/shard_map/dot_general | solution.py:656
  66.2 4.6 %fusion.32 = f32[1024,1536]{1,0:T(8,128)} fusion(bf16[1024,576]{1,0:T(8,128)(2,1)S(1)} %multiply_convert_fusion.2, bf16[576,1536]{1,0:T(8,128)(2,1)S(1)} %copy-done.24), kind=kOutput, calls=%fused_computation.199 | convolution fusion | flops 1811939328 | bytes 9240576 | tf_op jit(solution)/shard_map/dot_general | solution.py:657
  72.8 9.3 %multiply_convert_fusion = (bf16[1024,1536]{1,0:T(8,128)(2,1)}, bf16[1024,1536]{1,0:T(8,128)(2,1)}, bf16[1024,1536]{1,0:T(8,128)(2,1)S(1)}) fusion(f32[1024,1536]{1,0:T(8,128)} %fusion.31, f32[1024,1536]{1,0:T(8,128)} %fusion.32, bf16[1024,576]{1,0:T(8,128)(2,1)S(1)} %constant_dynamic-update-slice_fusion.3, bf16[1536,576]{0,1:T(8,128)(2,1)S(1)} %copy-done), kind=kOutput, calls=%fused_computation.4 | convolution fusion | flops 1837105152 | bytes 24969216 | tf_op jit(solution)/shard_map/dot_general | solution.py:51
  82.1 4.7 %fusion.33 = f32[1024,576]{1,0:T(8,128)S(1)} fusion(bf16[1024,1536]{1,0:T(8,128)(2,1)} %get-tuple-element.56, bf16[576,1536]{1,0:T(8,128)(2,1)S(1)} %copy-done.23), kind=kOutput, calls=%fused_computation.200 | convolution fusion | flops 1811939328 | bytes 7274496 | tf_op jit(solution)/shard_map/dot_general | solution.py:51
  88.9 3.8 %fusion.37 = f32[576,1536]{1,0:T(8,128)} fusion(bf16[1024,576]{1,0:T(8,128)(2,1)S(1)} %constant_dynamic-update-slice_fusion.3, bf16[1024,1536]{1,0:T(8,128)(2,1)S(1)} %get-tuple-element.57), kind=kOutput, calls=%fused_computation.204 | convolution fusion | flops 1811939328 | bytes 7864320 | tf_op jit(solution)/shard_map/dot_general | solution.py:45
  97.5 3.1 multiply_reduce_fusion
  103.7 15.1 %attend_back.1 = (bf16[576,1024]{1,0:T(8,128)(2,1)S(1)}, bf16[192,1024]{1,0:T(8,128)(2,1)S(1)}, bf16[192,1024]{1,0:T(8,128)(2,1)S(1)}) custom-call(bf16[576,1024]{1,0:T(8,128)(2,1)S(1)} %get-tuple-element.20.query_ref, bf16[192,1024]{1,0:T(8,128)(2,1)S(1)} %get-tuple-element.21.key_ref, bf16[192,1024]{1,0:T(8,128)(2,1)S(1)} %get-tuple-element.22.value_ref, ...), custom_call_target="tpu_custom_call" | custom-call | flops 24999999488 | bytes 8388608 | tf_op jit(solution)/shard_map/attend_back/pallas_call | solution.py:514
  135.8 16.8 %collective-permute-start.9 = (bf16[256,576]{1,0:T(8,128)(2,1)}, bf16[256,576]{1,0:T(8,128)(2,1)}, u32[]{:S(2)}, u32[]{:S(2)}) collective-permute-start(bf16[256,576]{1,0:T(8,128)(2,1)} %get-tuple-element.82), channel_id=1, source_target_pairs={{0,1},{1,2},{2,3},{3,0},{4,5},{5,6},{6,7},{7,4},{8,9},{9,10},{10,1... | collective-permute-start | bytes 884744 | tf_op jit(solution)/shard_map/ppermute | solution.py:608
  152.6 3.4 collective-permute-start.10
  158.2 14.6 %collective-permute-done.63 = f32[2,576]{1,0:T(2,128)S(1)} collective-permute-done((f32[2,576]{1,0:T(2,128)S(1)}, f32[2,576]{1,0:T(2,128)S(1)}, u32[]{:S(2)}, u32[]{:S(2)}) %collective-permute-start.63) | collective-permute-done | bytes 4640 | tf_op jit(solution)/shard_map/ppermute | solution.py:544
  172.8 4.3 %collective-permute-start.64 = (f32[2,576]{1,0:T(2,128)S(1)}, f32[2,576]{1,0:T(2,128)S(1)}, u32[]{:S(2)}, u32[]{:S(2)}) collective-permute-start(f32[2,576]{1,0:T(2,128)S(1)} %add.404), channel_id=1, source_target_pairs={{0,2},{1,3},{2,0},{3,1},{4,6},{5,7},{6,4},{7,5},{8,10},{9,11},{10,... | collective-permute-start | bytes 13832 | tf_op jit(solution)/shard_map/ppermute | solution.py:544
  178.2 5.2 %collective-permute-done.64 = f32[2,576]{1,0:T(2,128)S(1)} collective-permute-done((f32[2,576]{1,0:T(2,128)S(1)}, f32[2,576]{1,0:T(2,128)S(1)}, u32[]{:S(2)}, u32[]{:S(2)}) %collective-permute-start.64) | collective-permute-done | bytes 4640 | tf_op jit(solution)/shard_map/ppermute | solution.py:544
  183.5 4.0 %collective-permute-start.5 = (bf16[256,576]{1,0:T(8,128)(2,1)}, bf16[256,576]{1,0:T(8,128)(2,1)}, u32[]{:S(2)}, u32[]{:S(2)}) collective-permute-start(bf16[256,576]{1,0:T(8,128)(2,1)} %get-tuple-element.84), channel_id=1, source_target_pairs={{0,3},{1,0},{2,1},{3,2},{4,7},{5,4},{6,5},{7,6},{8,11},{9,8},{10,9... | collective-permute-start | bytes 884744 | tf_op jit(solution)/shard_map/ppermute | solution.py:608
  191.8 4.5 %collective-permute-done.3 = bf16[256,576]{1,0:T(8,128)(2,1)} collective-permute-done((bf16[256,576]{1,0:T(8,128)(2,1)}, bf16[256,576]{1,0:T(8,128)(2,1)}, u32[]{:S(2)}, u32[]{:S(2)}) %collective-permute-start.3) | collective-permute-done | bytes 294944 | tf_op jit(solution)/shard_map/ppermute | solution.py:608
  198.1 11.0 %collective-permute-done.4 = bf16[256,576]{1,0:T(8,128)(2,1)} collective-permute-done((bf16[256,576]{1,0:T(8,128)(2,1)}, bf16[256,576]{1,0:T(8,128)(2,1)}, u32[]{:S(2)}, u32[]{:S(2)}) %collective-permute-start.4) | collective-permute-done | bytes 294944 | tf_op jit(solution)/shard_map/ppermute | solution.py:608
  235.1 3.1 collective-permute-done.37
  239.6 4.8 %collective-permute-done.38 = bf16[72,1536]{1,0:T(8,128)(2,1)S(1)} collective-permute-done((bf16[72,1536]{1,0:T(8,128)(2,1)S(1)}, bf16[72,1536]{1,0:T(8,128)(2,1)S(1)}, u32[]{:S(2)}, u32[]{:S(2)}) %collective-permute-start.38) | collective-permute-done | bytes 221216 | tf_op jit(solution)/shard_map/ppermute | solution.py:544
  244.6 3.1 collective-permute-done.25
  249.1 4.7 %collective-permute-done.26 = bf16[72,1536]{1,0:T(8,128)(2,1)S(1)} collective-permute-done((bf16[72,1536]{1,0:T(8,128)(2,1)S(1)}, bf16[72,1536]{1,0:T(8,128)(2,1)S(1)}, u32[]{:S(2)}, u32[]{:S(2)}) %collective-permute-start.26) | collective-permute-done | bytes 221216 | tf_op jit(solution)/shard_map/ppermute | solution.py:544
  253.9 3.7 %collective-permute-start.52 = (bf16[72,768]{1,0:T(8,128)(2,1)S(1)}, bf16[72,768]{1,0:T(8,128)(2,1)S(1)}, u32[]{:S(2)}, u32[]{:S(2)}) collective-permute-start(bf16[72,768]{1,0:T(8,128)(2,1)S(1)} %dynamic-slice_convert_fusion.15), channel_id=1, source_target_pairs={{0,1},{1,0},{2,3},{3,2},{4,5},{5,4},{6,7},{7,6},{8,9},{9,8},{10,11... | collective-permute-start | bytes 331784 | tf_op jit(solution)/shard_map/ppermute | solution.py:544
  257.8 4.2 %collective-permute-start.28 = (bf16[72,768]{1,0:T(8,128)(2,1)S(1)}, bf16[72,768]{1,0:T(8,128)(2,1)S(1)}, u32[]{:S(2)}, u32[]{:S(2)}) collective-permute-start(bf16[72,768]{1,0:T(8,128)(2,1)S(1)} %dynamic-slice_convert_fusion.17), channel_id=1, source_target_pairs={{0,1},{1,0},{2,3},{3,2},{4,5},{5,4},{6,7},{7,6},{8,9},{9,8},{10,11... | collective-permute-start | bytes 331784 | tf_op jit(solution)/shard_map/ppermute | solution.py:544
  262.8 3.4 collective-permute-start.16
  266.2 3.1 collective-permute-start.53
  269.6 3.0 collective-permute-start.29
  272.9 2.8 collective-permute-start.54
  275.7 2.9 collective-permute-done.41
  306.1 2.9 collective-permute-done.44
  316.7 6.6 %collective-permute-done.20 = bf16[72,1536]{1,0:T(8,128)(2,1)S(1)} collective-permute-done((bf16[72,1536]{1,0:T(8,128)(2,1)S(1)}, bf16[72,1536]{1,0:T(8,128)(2,1)S(1)}, u32[]{:S(2)}, u32[]{:S(2)}) %collective-permute-start.20) | collective-permute-done | bytes 221216 | tf_op jit(solution)/shard_map/ppermute | solution.py:544
  324.9 6.6 %collective-permute-done.21 = bf16[72,1536]{1,0:T(8,128)(2,1)S(1)} collective-permute-done((bf16[72,1536]{1,0:T(8,128)(2,1)S(1)}, bf16[72,1536]{1,0:T(8,128)(2,1)S(1)}, u32[]{:S(2)}, u32[]{:S(2)}) %collective-permute-start.21) | collective-permute-done | bytes 221216 | tf_op jit(solution)/shard_map/ppermute | solution.py:544
  (308 shorter events, 168.5 us)
Async XLA Ops:
  5.3 26.5 %collective-permute-start = (bf16[256,576]{1,0:T(8,128)(2,1)}, bf16[256,576]{1,0:T(8,128)(2,1)}, u32[]{:S(2)}, u32[]{:S(2)}) collective-permute-start(bf16[256,576]{1,0:T(8,128)(2,1)} %bitcast.65), channel_id=1, source_target_pairs={{0,1},{1,2},{2,3},{3,0},{4,5},{5,6},{6,7},{7,4},{8,9},{9,10},{10,1... | collective-permute-start | bytes 884744 | tf_op jit(solution)/shard_map/ppermute | solution.py:595
  10.1 26.6 %collective-permute-start.1 = (bf16[256,576]{1,0:T(8,128)(2,1)}, bf16[256,576]{1,0:T(8,128)(2,1)}, u32[]{:S(2)}, u32[]{:S(2)}) collective-permute-start(bf16[256,576]{1,0:T(8,128)(2,1)} %bitcast.64), channel_id=1, source_target_pairs={{0,2},{1,3},{2,0},{3,1},{4,6},{5,7},{6,4},{7,5},{8,10},{9,11},{10,... | collective-permute-start | bytes 884744 | tf_op jit(solution)/shard_map/ppermute | solution.py:595
  14.6 23.9 %collective-permute-start.2 = (bf16[256,576]{1,0:T(8,128)(2,1)}, bf16[256,576]{1,0:T(8,128)(2,1)}, u32[]{:S(2)}, u32[]{:S(2)}) collective-permute-start(bf16[256,576]{1,0:T(8,128)(2,1)} %bitcast.63), channel_id=1, source_target_pairs={{0,3},{1,0},{2,1},{3,2},{4,7},{5,4},{6,5},{7,6},{8,11},{9,8},{10,9... | collective-permute-start | bytes 884744 | tf_op jit(solution)/shard_map/ppermute | solution.py:595
  16.8 53.9 %collective-permute-start.6 = (bf16[256,576]{1,0:T(8,128)(2,1)}, bf16[256,576]{1,0:T(8,128)(2,1)}, u32[]{:S(2)}, u32[]{:S(2)}) collective-permute-start(bf16[256,576]{1,0:T(8,128)(2,1)} %bitcast.62), channel_id=1, source_target_pairs={{0,1},{1,2},{2,3},{3,0},{4,5},{5,6},{6,7},{7,4},{8,9},{9,10},{10,1... | collective-permute-start | bytes 884744 | tf_op jit(solution)/shard_map/ppermute | solution.py:595
  18.4 53.3 %collective-permute-start.7 = (bf16[256,576]{1,0:T(8,128)(2,1)}, bf16[256,576]{1,0:T(8,128)(2,1)}, u32[]{:S(2)}, u32[]{:S(2)}) collective-permute-start(bf16[256,576]{1,0:T(8,128)(2,1)} %bitcast.16), channel_id=1, source_target_pairs={{0,2},{1,3},{2,0},{3,1},{4,6},{5,7},{6,4},{7,5},{8,10},{9,11},{10,... | collective-permute-start | bytes 884744 | tf_op jit(solution)/shard_map/ppermute | solution.py:595
  31.8 41.0 %collective-permute-start.8 = (bf16[256,576]{1,0:T(8,128)(2,1)}, bf16[256,576]{1,0:T(8,128)(2,1)S(1)}, u32[]{:S(2)}, u32[]{:S(2)}) collective-permute-start(bf16[256,576]{1,0:T(8,128)(2,1)} %bitcast.66), channel_id=1, source_target_pairs={{0,3},{1,0},{2,1},{3,2},{4,7},{5,4},{6,5},{7,6},{8,11},{9,8},{10,9... | collective-permute-start | bytes 884744 | tf_op jit(solution)/shard_map/ppermute | solution.py:595
  126.0 92.4 %collective-permute-start.48 = (bf16[288,1536]{1,0:T(8,128)(2,1)}, bf16[288,1536]{1,0:T(8,128)(2,1)}, u32[]{:S(2)}, u32[]{:S(2)}) collective-permute-start(bf16[288,1536]{1,0:T(8,128)(2,1)} %dynamic-slice_convert_fusion), channel_id=1, source_target_pairs={{0,4},{4,0},{8,12},{12,8},{16,20},{20,16},{24,28},{28,24},{1,5},{5... | collective-permute-start | bytes 2654216 | tf_op jit(solution)/shard_map/ppermute | solution.py:544
  133.0 22.9 %collective-permute-start.62 = (f32[2,576]{1,0:T(2,128)S(1)}, f32[2,576]{1,0:T(2,128)S(1)}, u32[]{:S(2)}, u32[]{:S(2)}) collective-permute-start(f32[2,576]{1,0:T(2,128)S(1)} %fusion.63), channel_id=1, source_target_pairs={{0,16},{4,20},{8,24},{12,28},{16,0},{20,4},{24,8},{28,12},{1,17},{... | collective-permute-start | bytes 13832 | tf_op jit(solution)/shard_map/ppermute | solution.py:544
  135.8 47.6 %collective-permute-start.9 = (bf16[256,576]{1,0:T(8,128)(2,1)}, bf16[256,576]{1,0:T(8,128)(2,1)}, u32[]{:S(2)}, u32[]{:S(2)}) collective-permute-start(bf16[256,576]{1,0:T(8,128)(2,1)} %get-tuple-element.82), channel_id=1, source_target_pairs={{0,1},{1,2},{2,3},{3,0},{4,5},{5,6},{6,7},{7,4},{8,9},{9,10},{10,1... | collective-permute-start | bytes 884744 | tf_op jit(solution)/shard_map/ppermute | solution.py:608
  152.6 30.9 %collective-permute-start.10 = (bf16[256,576]{1,0:T(8,128)(2,1)}, bf16[256,576]{1,0:T(8,128)(2,1)}, u32[]{:S(2)}, u32[]{:S(2)}) collective-permute-start(bf16[256,576]{1,0:T(8,128)(2,1)} %get-tuple-element.81), channel_id=1, source_target_pairs={{0,2},{1,3},{2,0},{3,1},{4,6},{5,7},{6,4},{7,5},{8,10},{9,11},{10,... | collective-permute-start | bytes 884744 | tf_op jit(solution)/shard_map/ppermute | solution.py:608
  156.0 34.6 %collective-permute-start.11 = (bf16[256,576]{1,0:T(8,128)(2,1)}, bf16[256,576]{1,0:T(8,128)(2,1)}, u32[]{:S(2)}, u32[]{:S(2)}) collective-permute-start(bf16[256,576]{1,0:T(8,128)(2,1)} %get-tuple-element.80), channel_id=1, source_target_pairs={{0,3},{1,0},{2,1},{3,2},{4,7},{5,4},{6,5},{7,6},{8,11},{9,8},{10,9... | collective-permute-start | bytes 884744 | tf_op jit(solution)/shard_map/ppermute | solution.py:608
  156.0 16.8 %collective-permute-start.63 = (f32[2,576]{1,0:T(2,128)S(1)}, f32[2,576]{1,0:T(2,128)S(1)}, u32[]{:S(2)}, u32[]{:S(2)}) collective-permute-start(f32[2,576]{1,0:T(2,128)S(1)} %add.403), channel_id=1, source_target_pairs={{0,1},{1,0},{2,3},{3,2},{4,5},{5,4},{6,7},{7,6},{8,9},{9,8},{10,11... | collective-permute-start | bytes 13832 | tf_op jit(solution)/shard_map/ppermute | solution.py:544
  183.4 25.7 %collective-permute-start.4 = (bf16[256,576]{1,0:T(8,128)(2,1)}, bf16[256,576]{1,0:T(8,128)(2,1)}, u32[]{:S(2)}, u32[]{:S(2)}) collective-permute-start(bf16[256,576]{1,0:T(8,128)(2,1)} %get-tuple-element.85), channel_id=1, source_target_pairs={{0,2},{1,3},{2,0},{3,1},{4,6},{5,7},{6,4},{7,5},{8,10},{9,11},{10,... | collective-permute-start | bytes 884744 | tf_op jit(solution)/shard_map/ppermute | solution.py:608
  183.5 27.4 %collective-permute-start.5 = (bf16[256,576]{1,0:T(8,128)(2,1)}, bf16[256,576]{1,0:T(8,128)(2,1)}, u32[]{:S(2)}, u32[]{:S(2)}) collective-permute-start(bf16[256,576]{1,0:T(8,128)(2,1)} %get-tuple-element.84), channel_id=1, source_target_pairs={{0,3},{1,0},{2,1},{3,2},{4,7},{5,4},{6,5},{7,6},{8,11},{9,8},{10,9... | collective-permute-start | bytes 884744 | tf_op jit(solution)/shard_map/ppermute | solution.py:608
  190.6 31.9 %collective-permute-start.36 = (bf16[288,1536]{1,0:T(8,128)(2,1)}, bf16[288,1536]{1,0:T(8,128)(2,1)}, u32[]{:S(2)}, u32[]{:S(2)}) collective-permute-start(bf16[288,1536]{1,0:T(8,128)(2,1)} %dynamic-slice_convert_fusion.1), channel_id=1, source_target_pairs={{0,4},{4,0},{8,12},{12,8},{16,20},{20,16},{24,28},{28,24},{1,5},{5... | collective-permute-start | bytes 2654216 | tf_op jit(solution)/shard_map/ppermute | solution.py:544
  196.2 29.4 %collective-permute-start.24 = (bf16[288,1536]{1,0:T(8,128)(2,1)}, bf16[288,1536]{1,0:T(8,128)(2,1)}, u32[]{:S(2)}, u32[]{:S(2)}) collective-permute-start(bf16[288,1536]{1,0:T(8,128)(2,1)} %dynamic-slice_convert_fusion.2), channel_id=1, source_target_pairs={{0,4},{4,0},{8,12},{12,8},{16,20},{20,16},{24,28},{28,24},{1,5},{5... | collective-permute-start | bytes 2654216 | tf_op jit(solution)/shard_map/ppermute | solution.py:544
  209.1 19.7 %collective-permute-start.12 = (bf16[288,1536]{1,0:T(8,128)(2,1)}, bf16[288,1536]{1,0:T(8,128)(2,1)}, u32[]{:S(2)}, u32[]{:S(2)}) collective-permute-start(bf16[288,1536]{1,0:T(8,128)(2,1)} %fusion.14), channel_id=1, source_target_pairs={{0,4},{4,0},{8,12},{12,8},{16,20},{20,16},{24,28},{28,24},{1,5},{5... | collective-permute-start | bytes 2654216 | tf_op jit(solution)/shard_map/ppermute | solution.py:544
  228.8 15.6 %collective-permute-start.38 = (bf16[72,1536]{1,0:T(8,128)(2,1)S(1)}, bf16[72,1536]{1,0:T(8,128)(2,1)S(1)}, u32[]{:S(2)}, u32[]{:S(2)}) collective-permute-start(bf16[72,1536]{1,0:T(8,128)(2,1)S(1)} %get-tuple-element.67), channel_id=1, source_target_pairs={{0,16},{4,20},{8,24},{12,28},{16,0},{20,4},{24,8},{28,12},{1,17},{... | collective-permute-start | bytes 663560 | tf_op jit(solution)/shard_map/ppermute | solution.py:544
  231.0 13.4 %collective-permute-start.39 = (bf16[72,1536]{1,0:T(8,128)(2,1)S(1)}, bf16[72,1536]{1,0:T(8,128)(2,1)S(1)}, u32[]{:S(2)}, u32[]{:S(2)}) collective-permute-start(bf16[72,1536]{1,0:T(8,128)(2,1)S(1)} %get-tuple-element.66), channel_id=1, source_target_pairs={{0,24},{4,28},{8,16},{12,20},{16,8},{20,12},{24,0},{28,4},{1,25},{... | collective-permute-start | bytes 663560 | tf_op jit(solution)/shard_map/ppermute | solution.py:544
  234.9 19.0 %collective-permute-start.26 = (bf16[72,1536]{1,0:T(8,128)(2,1)S(1)}, bf16[72,1536]{1,0:T(8,128)(2,1)S(1)}, u32[]{:S(2)}, u32[]{:S(2)}) collective-permute-start(bf16[72,1536]{1,0:T(8,128)(2,1)S(1)} %get-tuple-element.72), channel_id=1, source_target_pairs={{0,16},{4,20},{8,24},{12,28},{16,0},{20,4},{24,8},{28,12},{1,17},{... | collective-permute-start | bytes 663560 | tf_op jit(solution)/shard_map/ppermute | solution.py:544
  238.2 19.4 %collective-permute-start.27 = (bf16[72,1536]{1,0:T(8,128)(2,1)S(1)}, bf16[72,1536]{1,0:T(8,128)(2,1)S(1)}, u32[]{:S(2)}, u32[]{:S(2)}) collective-permute-start(bf16[72,1536]{1,0:T(8,128)(2,1)S(1)} %get-tuple-element.71), channel_id=1, source_target_pairs={{0,24},{4,28},{8,16},{12,20},{16,8},{20,12},{24,0},{28,4},{1,25},{... | collective-permute-start | bytes 663560 | tf_op jit(solution)/shard_map/ppermute | solution.py:544
  244.4 18.3 %collective-permute-start.14 = (bf16[72,1536]{1,0:T(8,128)(2,1)S(1)}, bf16[72,1536]{1,0:T(8,128)(2,1)S(1)}, u32[]{:S(2)}, u32[]{:S(2)}) collective-permute-start(bf16[72,1536]{1,0:T(8,128)(2,1)S(1)} %get-tuple-element.79), channel_id=1, source_target_pairs={{0,16},{4,20},{8,24},{12,28},{16,0},{20,4},{24,8},{28,12},{1,17},{... | collective-permute-start | bytes 663560 | tf_op jit(solution)/shard_map/ppermute | solution.py:544
  247.7 15.0 %collective-permute-start.15 = (bf16[72,1536]{1,0:T(8,128)(2,1)S(1)}, bf16[72,1536]{1,0:T(8,128)(2,1)S(1)}, u32[]{:S(2)}, u32[]{:S(2)}) collective-permute-start(bf16[72,1536]{1,0:T(8,128)(2,1)S(1)} %get-tuple-element.78), channel_id=1, source_target_pairs={{0,24},{4,28},{8,16},{12,20},{16,8},{20,12},{24,0},{28,4},{1,25},{... | collective-permute-start | bytes 663560 | tf_op jit(solution)/shard_map/ppermute | solution.py:544
  297.8 13.6 %collective-permute-start.45 = (bf16[72,1536]{1,0:T(8,128)(2,1)S(1)}, bf16[72,1536]{1,0:T(8,128)(2,1)S(1)}, u32[]{:S(2)}, u32[]{:S(2)}) collective-permute-start(bf16[72,1536]{1,0:T(8,128)(2,1)S(1)} %pad_maximum_fusion.7), channel_id=1, source_target_pairs={{0,16},{4,20},{8,24},{12,28},{16,0},{20,4},{24,8},{28,12},{1,17},{... | collective-permute-start | bytes 663560 | tf_op jit(solution)/shard_map/ppermute | solution.py:544
  299.5 14.5 %collective-permute-start.46 = (bf16[72,1536]{1,0:T(8,128)(2,1)S(1)}, bf16[72,1536]{1,0:T(8,128)(2,1)S(1)}, u32[]{:S(2)}, u32[]{:S(2)}) collective-permute-start(bf16[72,1536]{1,0:T(8,128)(2,1)S(1)} %pad_maximum_fusion.7), channel_id=1, source_target_pairs={{0,24},{4,28},{8,16},{12,20},{16,8},{20,12},{24,0},{28,4},{1,25},{... | collective-permute-start | bytes 663560 | tf_op jit(solution)/shard_map/ppermute | solution.py:544
  301.9 30.5 %collective-permute-start.32 = (bf16[72,1536]{1,0:T(8,128)(2,1)S(1)}, bf16[72,1536]{1,0:T(8,128)(2,1)S(1)}, u32[]{:S(2)}, u32[]{:S(2)}) collective-permute-start(bf16[72,1536]{1,0:T(8,128)(2,1)S(1)} %pad_maximum_fusion.6), channel_id=1, source_target_pairs={{0,8},{4,12},{8,0},{12,4},{16,24},{20,28},{24,16},{28,20},{1,9},{5... | collective-permute-start | bytes 663560 | tf_op jit(solution)/shard_map/ppermute | solution.py:544
  304.5 28.0 %collective-permute-start.33 = (bf16[72,1536]{1,0:T(8,128)(2,1)S(1)}, bf16[72,1536]{1,0:T(8,128)(2,1)S(1)}, u32[]{:S(2)}, u32[]{:S(2)}) collective-permute-start(bf16[72,1536]{1,0:T(8,128)(2,1)S(1)} %pad_maximum_fusion.6), channel_id=1, source_target_pairs={{0,16},{4,20},{8,24},{12,28},{16,0},{20,4},{24,8},{28,12},{1,17},{... | collective-permute-start | bytes 663560 | tf_op jit(solution)/shard_map/ppermute | solution.py:544
  309.0 14.3 %collective-permute-start.20 = (bf16[72,1536]{1,0:T(8,128)(2,1)S(1)}, bf16[72,1536]{1,0:T(8,128)(2,1)S(1)}, u32[]{:S(2)}, u32[]{:S(2)}) collective-permute-start(bf16[72,1536]{1,0:T(8,128)(2,1)S(1)} %pad_maximum_fusion.5), channel_id=1, source_target_pairs={{0,8},{4,12},{8,0},{12,4},{16,24},{20,28},{24,16},{28,20},{1,9},{5... | collective-permute-start | bytes 663560 | tf_op jit(solution)/shard_map/ppermute | solution.py:544
  311.4 20.2 %collective-permute-start.21 = (bf16[72,1536]{1,0:T(8,128)(2,1)S(1)}, bf16[72,1536]{1,0:T(8,128)(2,1)S(1)}, u32[]{:S(2)}, u32[]{:S(2)}) collective-permute-start(bf16[72,1536]{1,0:T(8,128)(2,1)S(1)} %pad_maximum_fusion.5), channel_id=1, source_target_pairs={{0,16},{4,20},{8,24},{12,28},{16,0},{20,4},{24,8},{28,12},{1,17},{... | collective-permute-start | bytes 663560 | tf_op jit(solution)/shard_map/ppermute | solution.py:544
  314.0 17.6 %collective-permute-start.22 = (bf16[72,1536]{1,0:T(8,128)(2,1)S(1)}, bf16[72,1536]{1,0:T(8,128)(2,1)S(1)}, u32[]{:S(2)}, u32[]{:S(2)}) collective-permute-start(bf16[72,1536]{1,0:T(8,128)(2,1)S(1)} %pad_maximum_fusion.5), channel_id=1, source_target_pairs={{0,24},{4,28},{8,16},{12,20},{16,8},{20,12},{24,0},{28,4},{1,25},{... | collective-permute-start | bytes 663560 | tf_op jit(solution)/shard_map/ppermute | solution.py:544
  331.6 17.2 %collective-permute-start.47 = (bf16[288,1536]{1,0:T(8,128)(2,1)}, bf16[288,1536]{1,0:T(8,128)(2,1)}, u32[]{:S(2)}, u32[]{:S(2)}) collective-permute-start(bf16[288,1536]{1,0:T(8,128)(2,1)} %pad_maximum_fusion.3), channel_id=1, source_target_pairs={{0,4},{4,0},{8,12},{12,8},{16,20},{20,16},{24,28},{28,24},{1,5},{5... | collective-permute-start | bytes 2654216 | tf_op jit(solution)/shard_map/ppermute | solution.py:544
  333.8 18.7 %collective-permute-start.35 = (bf16[288,1536]{1,0:T(8,128)(2,1)}, bf16[288,1536]{1,0:T(8,128)(2,1)}, u32[]{:S(2)}, u32[]{:S(2)}) collective-permute-start(bf16[288,1536]{1,0:T(8,128)(2,1)} %pad_maximum_fusion.2), channel_id=1, source_target_pairs={{0,4},{4,0},{8,12},{12,8},{16,20},{20,16},{24,28},{28,24},{1,5},{5... | collective-permute-start | bytes 2654216 | tf_op jit(solution)/shard_map/ppermute | solution.py:544
  (61 other events, 561.6 us)
